TPU v7x, 32 devices: a whole 2x2x4 slice. The times are simulated.
32 devices in a mesh: graph: 16 (over z, x, core), basis: 2 (over y).
Axes of the slice: x: 2, y: 2, z: 4, core: 2. Of those that a mesh axis runs over, the one named last changes fastest.
Arguments:
- edge_feats: bfloat16 [16384, 512], P(('graph', 'basis')), may hold values from -6 to 6
- pre_weight: bfloat16 [512, 512], replicated, may hold values from -0.25 to 0.25
- down_weight: bfloat16 [512, 64], replicated, may hold values from -0.25 to 0.25
- angle_tiles: bfloat16 [384, 2, 128, 128], P('graph', 'basis'), may hold values from -0.5 to 0.5
- part_source: int32 [384], P('graph'), may hold values from 0 to 7
- part_owner: int32 [384, 1], P('graph'), may hold values from 0 to 15; in each aligned block of 24 rows (0 to 23, 24 to 47, ...) at most 3 rows name the same one
- part_target: int32 [384], P('graph'), may hold values from 0 to 7
- up_weight: bfloat16 [2, 64, 512], P('basis'), may hold values from -0.5 to 0.5
- res_first: bfloat16 [512, 512], replicated, may hold values from -0.25 to 0.25
- res_second: bfloat16 [512, 512], replicated, may hold values from -0.25 to 0.25
- edge_slot: int32 [32, 512], P(('graph', 'basis')), may hold values from 0 to 127, never falling along the last dimension, each value on 1 to 8 neighbouring positions
- slot_owner: int32 [32, 128, 1], P(('graph', 'basis')), may hold values from 0 to 15; in each aligned block of 128 rows (0 to 127, 128 to 255, ..., all dimensions but the last counted through in order) at most 16 rows name the same one
- slot_atom: int32 [32, 128], P(('graph', 'basis')), may hold values from 0 to 31
- atom_feats: bfloat16 [1024, 512], P(('graph', 'basis')), may hold values from -6 to 6
- atom_first: bfloat16 [512, 512], replicated, may hold values from -0.25 to 0.25
- atom_second: bfloat16 [512, 512], replicated, may hold values from -0.25 to 0.25
Outputs:
- edge_update: bfloat16 [16384, 512], P(('graph', 'basis'))
- atom_update: bfloat16 [1024, 512], P(('graph', 'basis'))
Inputs may be any that keep to these rules, and one draw needn't show every extreme that they name: `part_owner`: the 24 parts of one graph shard name each shard at most 3 times, a bound that some block reaches. `slot_owner`: the 128 slots of one device name each graph shard at most 16 times, a bound that some block reaches. `edge_slot`: along a device's 512 rows the slot never falls; every slot holds 1 to 8 rows, one exactly 8.
All inputs are finite; a program needn't handle non-finite values.
Results may differ from a plain program's by a relative error of at most 0.015.
Values may be sent and summed in bfloat16 or wider, within the bound.
A program may use at most 64 MiB of HBM per device.

v0:
```python
import jax
import jax.numpy as jnp
from jax import lax
from jax.sharding import PartitionSpec as P

half_root = 0.5**0.5


def slot_ranks(target, peer_count, capacity):
    peer_ids = jnp.arange(peer_count, dtype=jnp.int32)
    picked = (target[:, None] == peer_ids[None, :]).astype(jnp.int32)
    earlier = jnp.cumsum(picked, axis=0) - picked
    return target * capacity + jnp.sum(earlier * picked, axis=1)


def slot_owners(positions, slot_total):
    places = jnp.arange(slot_total, dtype=jnp.int32)
    matches = positions[None, :] == places[:, None]
    filled = jnp.any(matches, axis=1)
    item_ids = jnp.arange(positions.shape[0], dtype=jnp.int32)
    owners = jnp.sum(jnp.where(matches, item_ids[None, :], 0), axis=1)
    return (owners, filled)


def body(
    edge_feats,
    pre_weight,
    down_weight,
    angle_tiles,
    part_source,
    part_owner,
    part_target,
    up_weight,
    res_first,
    res_second,
    edge_slot,
    slot_owner,
    slot_atom,
    atom_feats,
    atom_first,
    atom_second,
):
    block_rows = angle_tiles.shape[2]
    narrow = down_weight.shape[1]
    projected = jax.nn.silu(
        jnp.dot(edge_feats, pre_weight, preferred_element_type=jnp.float32)
    ).astype(jnp.bfloat16)
    lowered = jax.nn.silu(
        jnp.dot(projected, down_weight, preferred_element_type=jnp.float32)
    ).astype(jnp.bfloat16)
    shard_rows = lowered.shape[0]
    packed = lowered.reshape(shard_rows * narrow // 128, 128)
    whole_rows = lax.all_gather(packed, "basis", axis=0, tiled=True)
    blocks = whole_rows.reshape(-1, block_rows, narrow)
    count_blocks = blocks.shape[0]
    sources = blocks[part_source]
    products = jnp.einsum(
        "pij,pjk->pik", angle_tiles[:, 0], sources, preferred_element_type=jnp.float32
    ).astype(jnp.bfloat16)
    flat_products = products.reshape(products.shape[0], block_rows * narrow)
    peer_count = lax.axis_size("graph")
    parts_here = part_source.shape[0]
    capacity = max(2, 2 * parts_here // peer_count)
    positions = slot_ranks(part_owner[:, 0], peer_count, capacity)
    owners, filled = slot_owners(positions, peer_count * capacity)
    outgoing = jnp.where(filled[:, None], flat_products[owners], jnp.zeros((), jnp.bfloat16))
    out_target = jnp.where(filled, part_target[owners], -1)
    arrived, arrived_target = (
        lax.all_to_all(outgoing, "graph", split_axis=0, concat_axis=0, tiled=True),
        lax.all_to_all(out_target, "graph", split_axis=0, concat_axis=0, tiled=True),
    )
    block_ids = jnp.arange(count_blocks, dtype=jnp.int32)
    selector = (arrived_target[None, :] == block_ids[:, None]).astype(jnp.bfloat16)
    summed = jnp.dot(selector, arrived, preferred_element_type=jnp.float32)
    paired = summed.reshape(count_blocks * block_rows, narrow).astype(jnp.bfloat16)
    all_up = lax.all_gather(up_weight, "basis", axis=0, tiled=True)
    stacked = all_up.reshape(-1, all_up.shape[2])
    regrouped = lax.all_to_all(paired, "basis", split_axis=0, concat_axis=1, tiled=True)
    triplet = jnp.dot(regrouped, stacked, preferred_element_type=jnp.float32)
    joined = (edge_feats.astype(jnp.float32) + triplet).astype(jnp.bfloat16)
    inner_act = jax.nn.silu(jnp.dot(joined, res_first, preferred_element_type=jnp.float32)).astype(
        jnp.bfloat16
    )
    second = jax.nn.silu(jnp.dot(inner_act, res_second, preferred_element_type=jnp.float32))
    edge_update = ((joined.astype(jnp.float32) + second) * half_root).astype(jnp.bfloat16)
    slot_count = slot_owner.shape[1]
    slot_ids = jnp.arange(slot_count, dtype=jnp.int32)
    slot_select = (edge_slot[0][None, :] == slot_ids[:, None]).astype(jnp.bfloat16)
    slot_sums = jnp.dot(slot_select, edge_update, preferred_element_type=jnp.float32).astype(
        jnp.bfloat16
    )
    atom_cap = max(2, 2 * slot_count // peer_count)
    atom_places = slot_ranks(slot_owner[0, :, 0], peer_count, atom_cap)
    atom_owners, atom_filled = slot_owners(atom_places, peer_count * atom_cap)
    atom_out = jnp.where(atom_filled[:, None], slot_sums[atom_owners], jnp.zeros((), jnp.bfloat16))
    atom_target = jnp.where(atom_filled, slot_atom[0][atom_owners], -1)
    atom_arrived, atom_arrived_target = (
        lax.all_to_all(atom_out, "graph", split_axis=0, concat_axis=0, tiled=True),
        lax.all_to_all(atom_target, "graph", split_axis=0, concat_axis=0, tiled=True),
    )
    atom_ids = jnp.arange(atom_feats.shape[0], dtype=jnp.int32)
    atom_select = (atom_arrived_target[None, :] == atom_ids[:, None]).astype(jnp.bfloat16)
    gathered = jnp.dot(atom_select, atom_arrived, preferred_element_type=jnp.float32).astype(
        jnp.bfloat16
    )
    hidden = jax.nn.silu(jnp.dot(gathered, atom_first, preferred_element_type=jnp.float32)).astype(
        jnp.bfloat16
    )
    atom_update = (
        atom_feats.astype(jnp.float32)
        + jnp.dot(hidden, atom_second, preferred_element_type=jnp.float32)
    ).astype(jnp.bfloat16)
    return (edge_update, atom_update)


def solution(mesh):
    in_specs = (
        P(("graph", "basis"), None),
        P(),
        P(),
        P("graph", "basis", None, None),
        P("graph"),
        P("graph", None),
        P("graph"),
        P("basis", None, None),
        P(),
        P(),
        P(("graph", "basis"), None),
        P(("graph", "basis"), None, None),
        P(("graph", "basis"), None),
        P(("graph", "basis"), None),
        P(),
        P(),
    )
    out_specs = (P(("graph", "basis"), None), P(("graph", "basis"), None))
    return jax.shard_map(body, mesh=mesh, in_specs=in_specs, out_specs=out_specs, check_vma=False)
```

profile of v0, /device:TPU:0, one launch (start us, length us, event | category | flops | bytes accessed | tf_op | source)
XLA Modules:
  0.0 94.0 jit_solution(14485198151313465698)
XLA Ops:
  0.7 0.7 copy-done.11
  2.5 0.8 gather_fusion
  3.3 0.7 select_n.74
  4.0 7.4 %all-to-all-start = ((s32[16,3,1]{1,2,0:T(1,128)}), s32[16,3,1]{1,2,0:T(1,128)S(1)}, u32[]{:S(2)}, u32[]{:S(2)}) async-start(s32[16,3,1]{1,2,0:T(1,128)} %bitcast.3), calls=%async_computation | async-start | bytes 16384 | tf_op jit(solution)/shard_map/all_to_all | solution.py:70
  11.5 1.8 %multiply_convert_fusion.7 = bf16[512,64]{0,1:T(8,128)(2,1)S(1)} fusion(bf16[512,64]{0,1:T(8,128)(2,1)} %param.18, bf16[512,512]{1,0:T(8,128)(2,1)S(1)} %copy-done.6, bf16[512,512]{1,0:T(8,128)(2,1)} %param.17), kind=kOutput, calls=%fused_computation.30 | convolution fusion | flops 303464448 | bytes 1179648 | tf_op jit(solution)/shard_map/dot_general | solution.py:49
  13.6 5.1 %all_gather.6 = bf16[512,128]{1,0:T(8,128)(2,1)S(1)} all-gather(bf16[256,128]{1,0:T(8,128)(2,1)S(1)} %reshape.127), channel_id=1, replica_groups=mesh['graph'=16,'basis'=2] {'basis'}, dimensions={0}, use_global_device_ids=true | all-gather | bytes 196608 | tf_op jit(solution)/shard_map/all_gather | solution.py:53
  19.5 0.6 gather_fusion.1
  20.1 0.6 fusion.2
  21.2 0.6 reshape.129
  21.8 1.0 %gather_fusion.2 = bf16[48,8192]{1,0:T(8,128)(2,1)S(1)} fusion(bf16[24,8192]{1,0:T(8,128)(2,1)S(1)} %reshape.129, s32[1024]{0:T(1024)S(1)} %pad_clamp_fusion.2), kind=kCustom, calls=%fused_computation.2 | custom fusion | bytes 1573056 | tf_op jit(solution)/shard_map/gather | solution.py:66
  23.4 1.5 %broadcast_select_fusion = bf16[16,3,8192]{2,1,0:T(4,128)(2,1)} fusion(bf16[16,3,8192]{2,1,0:T(4,128)(2,1)S(1)} %gather.22, pred[16,3]{1,0:T(8,128)(4,1)S(1)} %broadcast_in_dim.85), kind=kLoop, calls=%fused_computation.19 | loop fusion | flops 393216 | bytes 1572912 | tf_op jit(solution)/shard_map/jit(_where)/select_n | solution.py:66
  24.9 5.8 %all-to-all-start.1 = ((bf16[16,3,8192]{2,1,0:T(4,128)(2,1)}), bf16[16,3,8192]{2,1,0:T(4,128)(2,1)S(1)}, u32[]{:S(2)}, u32[]{:S(2)}) async-start(bf16[16,3,8192]{2,1,0:T(4,128)(2,1)} %broadcast_select_fusion), calls=%async_computation.1 | async-start | bytes 2097152 | tf_op jit(solution)/shard_map/all_to_all | solution.py:69
  30.7 0.6 copy-done.10
  32.0 0.6 copy-done.1
  32.6 1.9 %gather_fusion.3 = s32[256]{0:T(256)S(1)} fusion(s32[128]{0:T(128)S(1)} %bitcast.46, s32[1024]{0:T(1024)S(1)} %pad_clamp_fusion), kind=kCustom, calls=%fused_computation.3 | custom fusion | bytes 3072 | tf_op jit(solution)/shard_map/gather | solution.py:96
  35.2 0.7 reduce.6
  36.0 17.6 %all-to-all-done.1 = bf16[16,3,8192]{2,1,0:T(4,128)(2,1)S(1)} async-done(((bf16[16,3,8192]{2,1,0:T(4,128)(2,1)}), bf16[16,3,8192]{2,1,0:T(4,128)(2,1)S(1)}, u32[]{:S(2)}, u32[]{:S(2)}) %all-to-all-start.1) | async-done | bytes 786464 | tf_op jit(solution)/shard_map/all_to_all | solution.py:69
  53.7 0.7 all_to_all.32
  54.8 0.8 copy.33
  55.6 3.5 %all-to-all-start.2 = ((bf16[2,512,64]{1,2,0:T(8,128)(2,1)}), bf16[2,512,64]{1,2,0:T(8,128)(2,1)S(1)}, u32[]{:S(2)}, u32[]{:S(2)}) async-start(bf16[2,512,64]{1,2,0:T(8,128)(2,1)} %copy.33), calls=%async_computation.2 | async-start | bytes 262144 | tf_op jit(solution)/shard_map/all_to_all | solution.py:78
  59.2 0.7 select_n.80
  59.9 5.4 %all_gather.7 = bf16[2,64,512]{2,1,0:T(8,128)(2,1)S(1)} all-gather(bf16[1,64,512]{2,1,0:T(8,128)(2,1)S(1)} %copy-done.7), channel_id=1, replica_groups=mesh['graph'=16,'basis'=2] {'basis'}, dimensions={0}, use_global_device_ids=true | all-gather | bytes 196608 | tf_op jit(solution)/shard_map/all_gather | solution.py:76
  65.3 6.6 %all-to-all-start.3 = ((s32[16,16,1]{1,2,0:T(1,128)}), s32[16,16,1]{1,2,0:T(1,128)S(1)}, u32[]{:S(2)}, u32[]{:S(2)}) async-start(s32[16,16,1]{1,2,0:T(1,128)} %bitcast.12), calls=%async_computation.3 | async-start | bytes 16384 | tf_op jit(solution)/shard_map/all_to_all | solution.py:99
  72.3 0.7 copy-done.12
  73.1 1.0 %multiply_convert_fusion = bf16[512,512]{1,0:T(8,128)(2,1)S(1)} fusion(bf16[512,512]{1,0:T(8,128)(2,1)S(1)} %fusion.1, bf16[512,512]{1,0:T(8,128)(2,1)S(1)} %copy-done.12, bf16[512,512]{1,0:T(8,128)(2,1)S(1)} %copy-done.13), kind=kOutput, calls=%fused_computation.16 | convolution fusion | flops 540278784 | bytes 2097152 | tf_op jit(solution)/shard_map/dot_general | solution.py:84
  74.4 1.2 %gather_fusion.4 = bf16[256,512]{1,0:T(8,128)(2,1)S(1)} fusion(bf16[128,512]{1,0:T(8,128)(2,1)S(1)} %convolution_convert_fusion.2, s32[1024]{0:T(1024)S(1)} %pad_clamp_fusion), kind=kCustom, calls=%fused_computation.4 | custom fusion | bytes 525312 | tf_op jit(solution)/shard_map/gather | solution.py:95
  75.6 0.8 broadcast_select_fusion.1
  76.4 1.8 %all-to-all-done.3 = s32[16,16,1]{1,2,0:T(1,128)S(1)} async-done(((s32[16,16,1]{1,2,0:T(1,128)}), s32[16,16,1]{1,2,0:T(1,128)S(1)}, u32[]{:S(2)}, u32[]{:S(2)}) %all-to-all-start.3) | async-done | bytes 1056 | tf_op jit(solution)/shard_map/all_to_all | solution.py:99
  78.2 4.2 %all-to-all-start.4 = ((bf16[16,16,512]{2,1,0:T(8,128)(2,1)}), bf16[16,16,512]{2,1,0:T(8,128)(2,1)S(1)}, u32[]{:S(2)}, u32[]{:S(2)}) async-start(bf16[16,16,512]{2,1,0:T(8,128)(2,1)} %broadcast_select_fusion.1), calls=%async_computation.4 | async-start | bytes 524288 | tf_op jit(solution)/shard_map/all_to_all | solution.py:98
  82.4 0.8 reduce.7
  83.3 9.2 %all-to-all-done.4 = bf16[16,16,512]{2,1,0:T(8,128)(2,1)S(1)} async-done(((bf16[16,16,512]{2,1,0:T(8,128)(2,1)}), bf16[16,16,512]{2,1,0:T(8,128)(2,1)S(1)}, u32[]{:S(2)}, u32[]{:S(2)}) %all-to-all-start.4) | async-done | bytes 262176 | tf_op jit(solution)/shard_map/all_to_all | solution.py:98
  93.2 0.8 fusion.3
  (64 shorter events, 6.6 us)
Async XLA Ops:
  0.6 19.5 %copy-start = (bf16[24,1,128,128]{3,2,1,0:T(8,128)(2,1)S(1)}, bf16[24,1,128,128]{3,2,1,0:T(8,128)(2,1)}, u32[]{:S(2)}) copy-start(bf16[24,1,128,128]{3,2,1,0:T(8,128)(2,1)} %param.19) | copy-start | bytes 2359300
  0.6 0.7 copy-start.11
  1.9 0.7 copy-start.2
  1.9 9.6 %copy-start.6 = (bf16[512,512]{1,0:T(8,128)(2,1)S(1)}, bf16[512,512]{1,0:T(8,128)(2,1)}, u32[]{:S(2)}) copy-start(bf16[512,512]{1,0:T(8,128)(2,1)} %param.16) | copy-start | bytes 1572868
  4.0 20.9 %all-to-all-start = ((s32[16,3,1]{1,2,0:T(1,128)}), s32[16,3,1]{1,2,0:T(1,128)S(1)}, u32[]{:S(2)}, u32[]{:S(2)}) async-start(s32[16,3,1]{1,2,0:T(1,128)} %bitcast.3), calls=%async_computation | async-start | bytes 16384 | tf_op jit(solution)/shard_map/all_to_all | solution.py:70
  18.8 0.7 copy-start.14
  24.9 28.8 %all-to-all-start.1 = ((bf16[16,3,8192]{2,1,0:T(4,128)(2,1)}), bf16[16,3,8192]{2,1,0:T(4,128)(2,1)S(1)}, u32[]{:S(2)}, u32[]{:S(2)}) async-start(bf16[16,3,8192]{2,1,0:T(4,128)(2,1)} %broadcast_select_fusion), calls=%async_computation.1 | async-start | bytes 2097152 | tf_op jit(solution)/shard_map/all_to_all | solution.py:69
  30.7 0.7 copy-start.10
  32.0 0.7 copy-start.1
  55.6 4.3 %copy-start.7 = (bf16[1,64,512]{2,1,0:T(8,128)(2,1)S(1)}, bf16[1,64,512]{2,1,0:T(8,128)(2,1)}, u32[]{:S(2)}) copy-start(bf16[1,64,512]{2,1,0:T(8,128)(2,1)} %param.23) | copy-start | bytes 196612
  55.6 9.7 %all-to-all-start.2 = ((bf16[2,512,64]{1,2,0:T(8,128)(2,1)}), bf16[2,512,64]{1,2,0:T(8,128)(2,1)S(1)}, u32[]{:S(2)}, u32[]{:S(2)}) async-start(bf16[2,512,64]{1,2,0:T(8,128)(2,1)} %copy.33), calls=%async_computation.2 | async-start | bytes 262144 | tf_op jit(solution)/shard_map/all_to_all | solution.py:78
  65.3 12.9 %all-to-all-start.3 = ((s32[16,16,1]{1,2,0:T(1,128)}), s32[16,16,1]{1,2,0:T(1,128)S(1)}, u32[]{:S(2)}, u32[]{:S(2)}) async-start(s32[16,16,1]{1,2,0:T(1,128)} %bitcast.12), calls=%async_computation.3 | async-start | bytes 16384 | tf_op jit(solution)/shard_map/all_to_all | solution.py:99
  71.9 1.0 %copy-start.12 = (bf16[512,512]{1,0:T(8,128)(2,1)S(1)}, bf16[512,512]{1,0:T(8,128)(2,1)}, u32[]{:S(2)}) copy-start(bf16[512,512]{1,0:T(8,128)(2,1)} %param.25) | copy-start | bytes 1572868
  71.9 1.2 %copy-start.13 = (bf16[512,512]{1,0:T(8,128)(2,1)S(1)}, bf16[512,512]{1,0:T(8,128)(2,1)}, u32[]{:S(2)}) copy-start(bf16[512,512]{1,0:T(8,128)(2,1)} %param.24) | copy-start | bytes 1572868
  73.1 1.1 %copy-start.9 = (s32[1,512]{1,0:T(1,128)S(1)}, s32[1,512]{1,0:T(1,128)}, u32[]{:S(2)}) copy-start(s32[1,512]{1,0:T(1,128)} %param.26) | copy-start | bytes 6148
  74.2 1.4 %copy-start.4 = (bf16[512,512]{1,0:T(8,128)(2,1)}, bf16[512,512]{1,0:T(8,128)(2,1)S(1)}, u32[]{:S(2)}) copy-start(bf16[512,512]{1,0:T(8,128)(2,1)S(1)} %multiply_convert_fusion) | copy-start | bytes 1572868
  75.6 16.9 %copy-start.3 = (bf16[512,512]{1,0:T(8,128)(2,1)S(1)}, bf16[512,512]{1,0:T(8,128)(2,1)}, u32[]{:S(2)}) copy-start(bf16[512,512]{1,0:T(8,128)(2,1)} %param.30) | copy-start | bytes 1572868
  78.2 14.2 %all-to-all-start.4 = ((bf16[16,16,512]{2,1,0:T(8,128)(2,1)}), bf16[16,16,512]{2,1,0:T(8,128)(2,1)S(1)}, u32[]{:S(2)}, u32[]{:S(2)}) async-start(bf16[16,16,512]{2,1,0:T(8,128)(2,1)} %broadcast_select_fusion.1), calls=%async_computation.4 | async-start | bytes 524288 | tf_op jit(solution)/shard_map/all_to_all | solution.py:98
  82.4 10.4 %copy-start.5 = (bf16[512,512]{1,0:T(8,128)(2,1)S(1)}, bf16[512,512]{1,0:T(8,128)(2,1)}, u32[]{:S(2)}) copy-start(bf16[512,512]{1,0:T(8,128)(2,1)} %param.31) | copy-start | bytes 1572868
  92.5 0.8 copy-start.8
where the time goes:
time: 94.8 us; the launch traced here: 94 us
  waiting for transfers between devices  28.7 us (30%)
  starting transfers between devices  27.4 us (29%)
  local copies, waits for them, and re-layouts  16 us (17%)
  blocking collectives  10.5 us (11%)
  matrix products  5.42 us (6%)
  other arithmetic  4.98 us (5%)
  between operations  1.02 us (1%)
    all_to_all x1, waiting for transfers between devices, body(): lax.all_to_all(outgoing, 'graph', split_axis=0, concat_axis=0, tiled=True)  17.6 us
    all_to_all x1, waiting for transfers between devices, body(): lax.all_to_all(atom_out, 'graph', split_axis=0, concat_axis=0, tiled=True)  9.18 us
    all_to_all x1, starting transfers between devices, body(): lax.all_to_all(out_target, 'graph', split_axis=0, concat_axis=0, tiled=True)  7.36 us
    all_to_all x1, starting transfers between devices, body(): lax.all_to_all(atom_target, 'graph', split_axis=0, concat_axis=0, tiled=T...  6.56 us
    all_to_all x1, starting transfers between devices, body(): lax.all_to_all(outgoing, 'graph', split_axis=0, concat_axis=0, tiled=True)  5.85 us
    all_gather x1, blocking collectives, body(): all_up = lax.all_gather(up_weight, 'basis', axis=0, tiled=True)  5.41 us
    all_gather x1, blocking collectives, body(): whole_rows = lax.all_gather(packed, 'basis', axis=0, tiled=True)  5.11 us
    unnamed x30, local copies, waits for them, and re-layouts  4.46 us
  transfers between devices with their start and end apart: 5, of which 3 were waited for; matrix products, arithmetic and copies ran while one was open for 18% of the time, Pallas kernels for 0%

commit v1 on v0

v1 whole, which is shorter than its diff:
```python
import functools

import jax
import jax.numpy as jnp
from jax import lax
from jax.experimental import pallas as pl
from jax.experimental.pallas import tpu as pltpu
from jax.sharding import PartitionSpec as P

half_root = 0.5**0.5
MESH = pl.DeviceIdType.MESH
bf16 = jnp.bfloat16
f32 = jnp.float32


def dot(a, b):
    return jnp.dot(a, b, preferred_element_type=f32)


def silu(v):
    return v / (1.0 + jnp.exp(-v))


def kernel(
    n, groups, cap, acap, parts, nb, block, tile_rows,
    scal, meta, owner_col, edge_slot,
    feats_h, pre_h, down_h, angle_h, up_h, first_h, second_h, afeats_h, afirst_h, asecond_h,
    edge_out, atom_out,
    feats, pre, down, angle, up_all, first, second, afeats, afirst, asecond,
    low_all, diag, prod, part_send, part_recv, meta_recv, acc, paired, pair_recv,
    atom_send, atom_recv,
    load_sem, meta_ss, meta_rs, part_ss, part_rs, atom_ss, atom_rs,
    low_ss, low_rs, up_ss, up_rs, pair_ss, pair_rs,
):
    me = lax.axis_index("graph")
    mine = lax.axis_index("basis")
    half = block // 2
    width = 2 * low_all.shape[3] // 2

    loads = [
        pltpu.make_async_copy(src, dst, load_sem.at[i])
        for i, (src, dst) in enumerate(
            [
                (feats_h, feats), (pre_h, pre), (down_h, down), (angle_h, angle),
                (up_h.at[0], up_all.at[mine]), (first_h, first), (second_h, second),
                (afeats_h, afeats), (afirst_h, afirst), (asecond_h, asecond),
            ]
        )
    ]
    for load in loads:
        load.start()

    barrier = pltpu.get_barrier_semaphore()

    def greet(k, carry):
        pl.semaphore_signal(
            barrier, inc=1, device_id=(lax.rem(me + k, n), mine), device_id_type=MESH
        )
        return carry

    lax.fori_loop(1, n, greet, 0)
    for k in range(1, groups):
        pl.semaphore_signal(
            barrier, inc=1, device_id=(me, lax.rem(mine + k, groups)), device_id_type=MESH
        )

    def send(src, dst, ss, rs, to, to_basis):
        return pltpu.make_async_remote_copy(
            src_ref=src, dst_ref=dst, send_sem=ss, recv_sem=rs,
            device_id=(to, to_basis), device_id_type=MESH,
        )

    def meta_copy(d, slot):
        return send(meta.at[d], meta_recv.at[slot], meta_ss.at[d], meta_rs.at[slot], d, mine)

    def part_copy(d, slot):
        return send(
            part_send.at[d], part_recv.at[slot], part_ss.at[d], part_rs.at[slot], d, mine
        )

    def atom_copy(d, slot):
        return send(
            atom_send.at[d], atom_recv.at[slot], atom_ss.at[d], atom_rs.at[slot], d, mine
        )

    def up_copy(g, slot):
        return send(up_h.at[0], up_all.at[slot], up_ss.at[g], up_rs.at[slot], me, g)

    def low_copy(g, slot):
        return send(low_all.at[mine], low_all.at[slot], low_ss.at[g], low_rs.at[slot], me, g)

    def pair_copy(g, slot):
        return send(paired.at[g], pair_recv.at[slot], pair_ss.at[g], pair_rs.at[slot], me, g)

    loads[0].wait()
    loads[1].wait()
    projected = silu(dot(feats[...], pre[...])).astype(bf16)
    loads[2].wait()
    down_twice = jnp.concatenate([down[...], down[...]], axis=1)
    lowered = silu(dot(projected, down_twice)).reshape(nb, 2, half, width)
    lane = lax.broadcasted_iota(jnp.int32, (nb, half, width), 2)
    low_all[mine] = jnp.where(lane < width // 2, lowered[:, 0], lowered[:, 1]).astype(bf16)

    pl.semaphore_wait(barrier, n - 1 + groups - 1)
    others = [lax.rem(mine + k, groups) for k in range(1, groups)]
    for g in others:
        low_copy(g, mine).start()

    def start_meta(k, carry):
        meta_copy(lax.rem(me + k, n), me).start()
        return carry

    lax.fori_loop(1, n, start_meta, 0)
    for g in others:
        up_copy(g, mine).start()
    meta_recv[me] = meta[me]

    def spread(g):
        lane = lax.broadcasted_iota(jnp.int32, (half, width), 1)
        left = lane < width // 2
        for i in range(nb):
            packed = low_all[g, i].astype(f32)
            turned = pltpu.roll(packed, width // 2, 1)
            at = g * nb + i
            diag[at, 0:half] = jnp.where(left, packed, 0.0).astype(bf16)
            diag[at, half : 2 * half] = jnp.where(left, turned, 0.0).astype(bf16)
            diag[at, 2 * half : 3 * half] = jnp.where(left, 0.0, turned).astype(bf16)
            diag[at, 3 * half :] = jnp.where(left, 0.0, packed).astype(bf16)

    spread(mine)
    loads[3].wait()
    for g in others:
        low_copy(g, g).wait_recv()
        spread(g)

    for p in range(parts):
        tile = angle[p, 0]
        wide = jnp.concatenate([tile[:half], tile[half:]], axis=1)
        prod[p] = dot(wide, diag[scal[p]]).astype(bf16)

    def fill(d, ref, slot):
        for s in range(cap):
            ref[slot, s] = prod[scal[parts + d * cap + s]]

    def start_part(i, carry):
        for k in (n // 2 + i, n // 2 - i):
            d = lax.rem(me + k, n)
            fill(d, part_send, d)
            part_copy(d, me).start()
        return carry

    d = lax.rem(me + n // 2, n)
    fill(d, part_send, d)
    part_copy(d, me).start()
    lax.fori_loop(1, n // 2, start_part, 0)
    fill(me, part_recv, me)

    acc[...] = jnp.zeros_like(acc)

    def add(src):
        targets = [meta_recv[src, s : s + 1, :] for s in range(cap)]
        arrived = [part_recv[src, s].astype(f32) for s in range(cap)]
        for j in range(groups * nb):
            total = acc[j]
            for t, a in zip(targets, arrived):
                total = total + jnp.where(jnp.broadcast_to(t == j, a.shape), a, 0.0)
            acc[j] = total

    add(me)

    def take(i, carry):
        src = lax.rem(me + i, n)
        meta_copy(src, src).wait_recv()
        part_copy(src, src).wait_recv()
        add(src)
        return carry

    lax.fori_loop(1, n, take, 0)

    rows_half = nb * half
    for g in range(groups):
        paired[g] = acc[g * nb : (g + 1) * nb].reshape(rows_half, width).astype(bf16)
    for g in others:
        pair_copy(g, mine).start()
    pair_recv[mine] = paired[mine]

    loads[4].wait()
    for g in others:
        up_copy(g, g).wait_recv()
    blank = jnp.zeros(up_all.shape[1:], bf16)
    above = jnp.concatenate([x for g in range(groups) for x in (up_all[g], blank)], axis=0)
    below = jnp.concatenate([x for g in range(groups) for x in (blank, up_all[g])], axis=0)
    pick = (owner_col[...] == edge_slot[...]).astype(f32).astype(bf16)
    loads[5].wait()
    loads[6].wait()
    for g in others:
        pair_copy(g, g).wait_recv()
    columns = jnp.concatenate([pair_recv[g] for g in range(groups)], axis=1)
    upper = dot(columns, above).reshape(nb, 1, half, above.shape[1])
    lower = dot(columns, below).reshape(nb, 1, half, above.shape[1])
    triplet = jnp.concatenate([upper, lower], axis=1).reshape(feats.shape)
    joined = (feats[...].astype(f32) + triplet).astype(bf16)
    inner = silu(dot(joined, first[...])).astype(bf16)
    deep = silu(dot(inner, second[...]))
    update = ((joined.astype(f32) + deep) * half_root).astype(bf16)
    edge_out[...] = update

    atom_send[...] = dot(pick, update).astype(bf16).reshape(atom_send.shape)

    def start_atom(i, carry):
        for k in (n // 2 + i, n // 2 - i):
            atom_copy(lax.rem(me + k, n), me).start()
        return carry

    atom_copy(lax.rem(me + n // 2, n), me).start()
    lax.fori_loop(1, n // 2, start_atom, 0)
    atom_recv[me] = atom_send[me]

    named = jnp.sum(meta_recv[...], axis=0)[tile_rows:]
    atoms = afeats.shape[0]
    chunks = n * acap // 128
    ids = lax.broadcasted_iota(jnp.int32, (atoms, 128), 0) + 1
    chosen = jnp.concatenate(
        [(ids == named[r : r + 1]).astype(f32).astype(bf16) for r in range(chunks)], axis=1
    )
    for load in loads[7:]:
        load.wait()

    def take_atom(i, carry):
        src = lax.rem(me + i, n)
        atom_copy(src, src).wait_recv()
        return carry

    lax.fori_loop(1, n, take_atom, 0)
    gathered = dot(chosen, atom_recv[...].reshape(n * acap, atom_recv.shape[2])).astype(bf16)
    hidden = silu(dot(gathered, afirst[...])).astype(bf16)
    atom_out[...] = (afeats[...].astype(f32) + dot(hidden, asecond[...])).astype(bf16)

    def finish(k, carry):
        d = lax.rem(me + k, n)
        meta_copy(d, me).wait_send()
        part_copy(d, me).wait_send()
        atom_copy(d, me).wait_send()
        return carry

    lax.fori_loop(1, n, finish, 0)
    for g in others:
        low_copy(g, mine).wait_send()
        up_copy(g, mine).wait_send()
        pair_copy(g, mine).wait_send()


def slot_table(target, peers, capacity, stride, values):
    count = target.shape[0]
    ids = jnp.arange(count, dtype=jnp.int32)
    same = (target[:, None] == target[None, :]) & (ids[None, :] < ids[:, None])
    rank = jnp.sum(same.astype(jnp.int32), axis=1)
    place = target * stride + rank
    slots = jnp.arange(peers * stride, dtype=jnp.int32)
    match = place[None, :] == slots[:, None]
    items = jnp.sum(jnp.where(match, ids[None, :] + 1, 0), axis=1) - 1
    picked = jnp.sum(jnp.where(match, values[None, :] + 1, 0), axis=1) - 1
    return items, picked


def body(
    edge_feats, pre_weight, down_weight, angle_tiles, part_source, part_owner, part_target,
    up_weight, res_first, res_second, edge_slot, slot_owner, slot_atom, atom_feats,
    atom_first, atom_second,
):
    n, groups = lax.axis_size("graph"), lax.axis_size("basis")
    me = lax.axis_index("graph")
    parts, _, block, _ = angle_tiles.shape
    narrow = down_weight.shape[1]
    rows, wide = edge_feats.shape
    nb = rows // block
    slot_count = slot_owner.shape[1]
    cap = max(2, 2 * parts // n)
    acap = -(-max(2, 2 * slot_count // n) // 16) * 16

    items, targets = slot_table(part_owner[:, 0], n, cap, cap, part_target)
    scal = jnp.concatenate([part_source, jnp.maximum(items, 0)])
    owners, atoms = slot_table(slot_owner[0, :, 0], n, acap, acap, slot_atom[0])
    tile_rows = cap
    chunk_rows = n * acap // 128
    rows_meta = -(-(cap + chunk_rows) // 8) * 8
    part_rows = jnp.broadcast_to(targets.reshape(n, cap, 1), (n, cap, 128))
    seat = jnp.arange(n, dtype=jnp.int32)[None, :, None] == me
    atom_rows = jnp.where(seat, atoms.reshape(n, 1, acap) + 1, 0).reshape(n, chunk_rows, 128)
    meta = jnp.concatenate(
        [part_rows, atom_rows, jnp.zeros((n, rows_meta - cap - chunk_rows, 128), jnp.int32)],
        axis=1,
    )

    half, pair_width = block // 2, 2 * narrow
    dma = pltpu.SemaphoreType.DMA
    vmem = pl.BlockSpec(memory_space=pltpu.VMEM)
    hbm = pl.BlockSpec(memory_space=pl.ANY)
    scratch = [
        pltpu.VMEM(edge_feats.shape, bf16),
        pltpu.VMEM(pre_weight.shape, bf16),
        pltpu.VMEM(down_weight.shape, bf16),
        pltpu.VMEM(angle_tiles.shape, bf16),
        pltpu.VMEM((groups,) + up_weight.shape[1:], bf16),
        pltpu.VMEM(res_first.shape, bf16),
        pltpu.VMEM(res_second.shape, bf16),
        pltpu.VMEM(atom_feats.shape, bf16),
        pltpu.VMEM(atom_first.shape, bf16),
        pltpu.VMEM(atom_second.shape, bf16),
        pltpu.VMEM((groups, nb, half, pair_width), bf16),
        pltpu.VMEM((groups * nb, 2 * block, pair_width), bf16),
        pltpu.VMEM((parts, half, pair_width), bf16),
        pltpu.VMEM((n, cap, half, pair_width), bf16),
        pltpu.VMEM((n, cap, half, pair_width), bf16),
        pltpu.VMEM((n, rows_meta, 128), jnp.int32),
        pltpu.VMEM((groups * nb, half, pair_width), f32),
        pltpu.VMEM((groups, nb * half, pair_width), bf16),
        pltpu.VMEM((groups, nb * half, pair_width), bf16),
        pltpu.VMEM((n, acap, wide), bf16),
        pltpu.VMEM((n, acap, wide), bf16),
        dma((10,)),
    ] + [dma((n,))] * 6 + [dma((groups,))] * 6
    return pl.pallas_call(
        functools.partial(kernel, n, groups, cap, acap, parts, nb, block, tile_rows),
        out_shape=(
            jax.ShapeDtypeStruct(edge_feats.shape, bf16),
            jax.ShapeDtypeStruct(atom_feats.shape, bf16),
        ),
        in_specs=[pl.BlockSpec(memory_space=pltpu.SMEM), vmem, vmem, vmem] + [hbm] * 10,
        out_specs=(vmem, vmem),
        scratch_shapes=scratch,
        compiler_params=pltpu.CompilerParams(
            collective_id=0, has_side_effects=True, vmem_limit_bytes=40 * 2**20
        ),
    )(
        scal, meta, owners[:, None], edge_slot, edge_feats, pre_weight, down_weight,
        angle_tiles, up_weight, res_first, res_second, atom_feats, atom_first, atom_second,
    )


def solution(mesh):
    rows = P(("graph", "basis"), None)
    in_specs = (
        rows,
        P(),
        P(),
        P("graph", "basis", None, None),
        P("graph"),
        P("graph", None),
        P("graph"),
        P("basis", None, None),
        P(),
        P(),
        rows,
        P(("graph", "basis"), None, None),
        rows,
        rows,
        P(),
        P(),
    )
    return jax.shard_map(
        body, mesh=mesh, in_specs=in_specs, out_specs=(rows, rows), check_vma=False
    )
```

time: 94.8 us -> 58.5 us (0.62)
  Pallas kernels: 0 us -> 42.2 us
  waiting for transfers between devices: 28.7 us -> 0 us
  starting transfers between devices: 27.4 us -> 0 us
  blocking collectives: 10.5 us -> 0 us
  local copies, waits for them, and re-layouts: 16 us -> 9.41 us
  matrix products: 5.42 us -> 0 us
    pallas_call x0 -> x1, Pallas kernels: none -> 42.2 us  [body(): pl.pallas_call(functools.partial(kernel, n, groups, cap, acap, parts, nb,...]
    all_to_all x5 -> x0, waiting for transfers between devices: 28.7 us -> none  [the longest x1 17.6 us: body(): lax.all_to_all(outgoing, 'graph', split_axis=0, concat_axis=0, tiled=True)]
    all_to_all x5 -> x0, starting transfers between devices: 27.4 us -> none  [the longest x1 7.36 us: body(): lax.all_to_all(out_target, 'graph', split_axis=0, concat_axis=0, tiled=True)]
    all_gather x2 -> x0, blocking collectives: 10.5 us -> none  [the longest x1 5.41 us: body(): all_up = lax.all_gather(up_weight, 'basis', axis=0, tiled=True)]
    gather x6 -> x0, local copies, waits for them, and re-layouts: 5.95 us -> none  [the longest x1 1.87 us: body(): atom_target = jnp.where(atom_filled, slot_atom[0][atom_owners], -1)]
    dot_general x8 -> x0, matrix products: 5.42 us -> none  [the longest x1 1.84 us: body(): jnp.dot(projected, down_weight, preferred_element_type=jnp.float32)]
    unnamed x30 -> x23, local copies, waits for them, and re-layouts: 4.46 us -> 8.66 us
    select_n x7 -> x1, other arithmetic: 2.32 us -> 0.01 us  [body(): jnp.where(seat, atoms.reshape(n, 1, acap) + 1, 0)]
  transfers between devices with their start and end apart: 5 -> 0, of which waited for: 3 -> 0; matrix products, arithmetic and copies ran while one was open for 18% -> 0% of each run, Pallas kernels for 0% -> 0%
where the time goes in v1:
time: 58.5 us; the launch traced here: 58 us
  Pallas kernels  42.2 us (72%)
  local copies, waits for them, and re-layouts  9.41 us (16%)
  other arithmetic  5.6 us (10%)
  between operations  0.79 us (1%)
    pallas_call x1, Pallas kernels, body(): pl.pallas_call(functools.partial(kernel, n, groups, cap, acap, parts, nb,...  42.2 us
    unnamed x23, local copies, waits for them, and re-layouts  8.66 us
    reduce_sum x2, other arithmetic, slot_table(): rank = jnp.sum(same.astype(jnp.int32), axis=1)  1.81 us

profile of v1, /device:TPU:0, one launch (start us, length us, event | category | flops | bytes accessed | tf_op | source)
XLA Modules:
  0.0 58.0 jit_solution(13736833034471231817)
XLA Ops:
  0.7 0.7 %broadcast_add_fusion.2 = s32[24]{0:T(128)S(1)} fusion(s32[24]{0:T(128)} %param.22), kind=kLoop, calls=%fused_computation.24 | loop fusion | flops 24 | bytes 192 | tf_op jit(solution)/shard_map/add | solution.py:262
  1.4 0.7 %add_bitcast_fusion = s32[128]{0:T(128)S(1)} fusion(s32[1,128]{1,0:T(1,128)} %param.28), kind=kLoop, calls=%fused_computation.18 | loop fusion | flops 128 | bytes 1024 | tf_op jit(solution)/shard_map/jit(_where)/broadcast_in_dim | solution.py:262
  2.0 0.9 %convert_reduce_fusion = s32[128]{0:T(128)S(1)} fusion(s32[128]{0:T(128)} %bitcast.8), kind=kLoop, calls=%fused_computation.4 | loop fusion | flops 81792 | bytes 1024 | tf_op jit(solution)/shard_map/reduce_sum | solution.py:257
  2.9 0.9 %convert_reduce_fusion.1 = s32[24]{0:T(128)S(1)} fusion(s32[24]{0:T(128)} %bitcast.9), kind=kLoop, calls=%fused_computation.11 | loop fusion | flops 2856 | bytes 192 | tf_op jit(solution)/shard_map/reduce_sum | solution.py:257
  3.9 0.7 %multiply_add_fusion.1 = s32[24]{0:T(128)S(1)} fusion(s32[24]{0:T(128)S(1)} %convert_reduce_fusion.1, s32[24,1]{0,1:T(1,128)} %param.21), kind=kLoop, calls=%fused_computation.22 | loop fusion | flops 48 | bytes 288 | tf_op jit(solution)/shard_map/add | solution.py:258
  4.5 0.1 pad.2.clone
  4.6 0.1 select_reduce_fusion.2
  4.7 0.7 %pad_add_fusion.scal = s32[72]{0:T(128)S(1)} fusion(s32[48]{0:T(128)S(1)} %get-tuple-element.6, s32[24]{0:T(128)} %param.20), kind=kLoop, calls=%fused_computation.15 | loop fusion | flops 72 | bytes 576 | tf_op jit(solution)/shard_map/concatenate | solution.py:282
  5.5 0.7 %iota_add_fusion = (s32[128]{0:T(128)S(1)}, s32[128]{0:T(128)S(1)}) fusion(s32[128]{0:T(128)S(1)} %convert_reduce_fusion, s32[1,128,1]{1,2,0:T(1,128)} %param.27), kind=kLoop, calls=%fused_computation.17 | loop fusion | flops 384 | bytes 2048 | tf_op jit(solution)/shard_map/add | solution.py:261
  6.1 0.2 select_reduce_fusion
  6.3 0.1 broadcast_in_dim.89
  6.3 0.1 broadcast_in_dim.90
  6.4 0.1 reduce_sum.61
  6.5 0.1 sub.16
  6.6 0.1 broadcast_in_dim.88
  6.7 0.1 broadcast_in_dim.96
  6.8 0.1 add_add_fusion.meta
  6.9 0.1 copy.21.owner_col
  7.1 0.0 copy-start.7
  7.1 0.0 copy-start.8
  7.1 0.0 copy-start.9
  7.1 1.0 %copy.22.down_h = bf16[512,64]{1,0:T(8,128)(2,1)S(1)} copy(bf16[512,64]{0,1:T(8,128)(2,1)} %param.18) | data formatting | bytes 131072 | tf_op args[2]
  8.1 0.0 copy-start.1
  8.1 1.0 %copy-done.1 = bf16[512,512]{1,0:T(8,128)(2,1)S(1)} copy-done((bf16[512,512]{1,0:T(8,128)(2,1)S(1)}, bf16[512,512]{1,0:T(8,128)(2,1)}, u32[]{:S(2)}) %copy-start.1) | copy-done | bytes 524312
  9.2 1.0 %copy-done.2 = bf16[512,512]{1,0:T(8,128)(2,1)S(1)} copy-done((bf16[512,512]{1,0:T(8,128)(2,1)S(1)}, bf16[512,512]{1,0:T(8,128)(2,1)}, u32[]{:S(2)}) %copy-start.2) | copy-done | bytes 524312
  10.2 1.0 %copy-done.3 = bf16[512,512]{1,0:T(8,128)(2,1)S(1)} copy-done((bf16[512,512]{1,0:T(8,128)(2,1)S(1)}, bf16[512,512]{1,0:T(8,128)(2,1)}, u32[]{:S(2)}) %copy-start.3) | copy-done | bytes 524312
  11.3 1.0 %copy-done.4 = bf16[512,512]{1,0:T(8,128)(2,1)S(1)} copy-done((bf16[512,512]{1,0:T(8,128)(2,1)S(1)}, bf16[512,512]{1,0:T(8,128)(2,1)}, u32[]{:S(2)}) %copy-start.4) | copy-done | bytes 524312
  12.3 1.0 %copy-done.5 = bf16[512,512]{1,0:T(8,128)(2,1)S(1)} copy-done((bf16[512,512]{1,0:T(8,128)(2,1)S(1)}, bf16[512,512]{1,0:T(8,128)(2,1)}, u32[]{:S(2)}) %copy-start.5) | copy-done | bytes 524312
  13.3 1.0 %copy-done.6 = bf16[512,512]{1,0:T(8,128)(2,1)S(1)} copy-done((bf16[512,512]{1,0:T(8,128)(2,1)S(1)}, bf16[512,512]{1,0:T(8,128)(2,1)}, u32[]{:S(2)}) %copy-start.6) | copy-done | bytes 524312
  14.4 42.2 %shard_map.167 = (bf16[512,512]{1,0:T(8,128)(2,1)S(1)}, bf16[32,512]{1,0:T(8,128)(2,1)S(1)}) custom-call(s32[72]{0:T(128)S(1)} %pad_add_fusion.scal, s32[16,8,128]{2,1,0:T(8,128)S(1)} %add_add_fusion.meta, s32[256,1]{1,0:T(8,128)S(1)} %copy.21.owner_col, s32[1,512]{1,0:T(1,128)S(1)} %copy-done.9, bf16[512,512]{1,0:T(8,128)(2,1)S(1)} %copy-done.1, ...), custom_call_target="tpu_custom_call" | custom-call | tf_op jit(solution)/shard_map/pallas_call | solution.py:323
  56.5 0.8 %copy.25 = bf16[512,512]{1,0:T(8,128)(2,1)} copy(bf16[512,512]{1,0:T(8,128)(2,1)S(1)} %get-tuple-element.12) | data formatting | bytes 1048576
  57.3 0.6 %copy.26 = bf16[32,512]{1,0:T(8,128)(2,1)} copy(bf16[32,512]{1,0:T(8,128)(2,1)S(1)} %get-tuple-element.13) | data formatting | bytes 65536
  (17 shorter events, 0.1 us)
Async XLA Ops:
  0.6 7.5 %copy-start = (bf16[24,1,128,128]{3,2,1,0:T(8,128)(2,1)S(1)}, bf16[24,1,128,128]{3,2,1,0:T(8,128)(2,1)}, u32[]{:S(2)}) copy-start(bf16[24,1,128,128]{3,2,1,0:T(8,128)(2,1)} %angle_h.1) | copy-start | bytes 2359300
  7.1 1.0 %copy-start.7 = (bf16[1,64,512]{2,1,0:T(8,128)(2,1)S(1)}, bf16[1,64,512]{2,1,0:T(8,128)(2,1)}, u32[]{:S(2)}) copy-start(bf16[1,64,512]{2,1,0:T(8,128)(2,1)} %up_h.1) | copy-start | bytes 196612
  7.1 1.0 %copy-start.8 = (bf16[32,512]{1,0:T(8,128)(2,1)S(1)}, bf16[32,512]{1,0:T(8,128)(2,1)}, u32[]{:S(2)}) copy-start(bf16[32,512]{1,0:T(8,128)(2,1)} %afeats_h.1) | copy-start | bytes 98308
  7.1 1.0 %copy-start.9 = (s32[1,512]{1,0:T(1,128)S(1)}, s32[1,512]{1,0:T(1,128)}, u32[]{:S(2)}) copy-start(s32[1,512]{1,0:T(1,128)} %edge_slot.1) | copy-start | bytes 6148
  8.1 1.0 %copy-start.1 = (bf16[512,512]{1,0:T(8,128)(2,1)S(1)}, bf16[512,512]{1,0:T(8,128)(2,1)}, u32[]{:S(2)}) copy-start(bf16[512,512]{1,0:T(8,128)(2,1)} %feats_h.1) | copy-start | bytes 1572868
  9.2 1.0 %copy-start.2 = (bf16[512,512]{1,0:T(8,128)(2,1)S(1)}, bf16[512,512]{1,0:T(8,128)(2,1)}, u32[]{:S(2)}) copy-start(bf16[512,512]{1,0:T(8,128)(2,1)} %pre_h.1) | copy-start | bytes 1572868
  10.2 1.0 %copy-start.3 = (bf16[512,512]{1,0:T(8,128)(2,1)S(1)}, bf16[512,512]{1,0:T(8,128)(2,1)}, u32[]{:S(2)}) copy-start(bf16[512,512]{1,0:T(8,128)(2,1)} %first_h.1) | copy-start | bytes 1572868
  11.3 1.0 %copy-start.4 = (bf16[512,512]{1,0:T(8,128)(2,1)S(1)}, bf16[512,512]{1,0:T(8,128)(2,1)}, u32[]{:S(2)}) copy-start(bf16[512,512]{1,0:T(8,128)(2,1)} %second_h.1) | copy-start | bytes 1572868
  12.3 1.0 %copy-start.5 = (bf16[512,512]{1,0:T(8,128)(2,1)S(1)}, bf16[512,512]{1,0:T(8,128)(2,1)}, u32[]{:S(2)}) copy-start(bf16[512,512]{1,0:T(8,128)(2,1)} %afirst_h.1) | copy-start | bytes 1572868
  13.3 1.0 %copy-start.6 = (bf16[512,512]{1,0:T(8,128)(2,1)S(1)}, bf16[512,512]{1,0:T(8,128)(2,1)}, u32[]{:S(2)}) copy-start(bf16[512,512]{1,0:T(8,128)(2,1)} %asecond_h.1) | copy-start | bytes 1572868

commit v2 on v1

v2 whole, which is shorter than its diff:
```python
import functools

import jax
import jax.numpy as jnp
from jax import lax
from jax.experimental import pallas as pl
from jax.experimental.pallas import tpu as pltpu
from jax.sharding import PartitionSpec as P

half_root = 0.5**0.5
MESH = pl.DeviceIdType.MESH
bf16 = jnp.bfloat16
f32 = jnp.float32


def dot(a, b):
    return jnp.dot(a, b, preferred_element_type=f32)


def silu(v):
    return v / (1.0 + jnp.exp(-v))


def lines(shape, axis):
    return lax.broadcasted_iota(jnp.int32, shape, axis)


def ranks(row):
    count = row.shape[1]
    down, along = lines((count, count), 0), lines((count, count), 1)
    col = jnp.sum(jnp.where(down == along, row, 0), axis=1, keepdims=True)
    same = jnp.where(col == row, 1, 0)
    rank_row = jnp.sum(jnp.where(down < along, same, 0), axis=0, keepdims=True)
    rank_col = jnp.sum(jnp.where(along < down, same, 0), axis=1, keepdims=True)
    return col, rank_row, rank_col


def kernel(
    n, groups, cap, acap, seat, chunks, nb, block,
    part_source, part_owner, part_target, slot_owner, slot_atom, edge_slot,
    feats_h, pre_h, down_h, angle_h, up_h, first_h, second_h, afeats_h, afirst_h, asecond_h,
    edge_out, atom_out,
    feats, pre, down, angle, up_all, first, second, afeats, afirst, asecond,
    low_all, diag, prod, part_send, part_recv, meta, meta_recv, items_v, items, acc, paired,
    pair_recv, pick, atom_send, atom_recv,
    load_sem, item_sem, meta_ss, meta_rs, part_ss, part_rs, atom_ss, atom_rs,
    low_ss, low_rs, up_ss, up_rs, pair_ss, pair_rs,
):
    me = lax.axis_index("graph")
    mine = lax.axis_index("basis")
    half = block // 2
    width = 2 * low_all.shape[3] // 2

    loads = [
        pltpu.make_async_copy(src, dst, load_sem.at[i])
        for i, (src, dst) in enumerate(
            [
                (feats_h, feats), (pre_h, pre), (down_h, down), (angle_h, angle),
                (up_h.at[0], up_all.at[mine]), (first_h, first), (second_h, second),
                (afeats_h, afeats), (afirst_h, afirst), (asecond_h, asecond),
            ]
        )
    ]
    for load in loads:
        load.start()

    barrier = pltpu.get_barrier_semaphore()

    def greet(k, carry):
        pl.semaphore_signal(
            barrier, inc=1, device_id=(lax.rem(me + k, n), mine), device_id_type=MESH
        )
        return carry

    lax.fori_loop(1, n, greet, 0)
    for k in range(1, groups):
        pl.semaphore_signal(
            barrier, inc=1, device_id=(me, lax.rem(mine + k, groups)), device_id_type=MESH
        )

    def send(src, dst, ss, rs, to, to_basis):
        return pltpu.make_async_remote_copy(
            src_ref=src, dst_ref=dst, send_sem=ss, recv_sem=rs,
            device_id=(to, to_basis), device_id_type=MESH,
        )

    def meta_copy(d, slot):
        return send(meta.at[d], meta_recv.at[slot], meta_ss.at[d], meta_rs.at[slot], d, mine)

    def part_copy(h, d, slot):
        return send(
            part_send.at[h, d], part_recv.at[h, slot], part_ss.at[h, d], part_rs.at[h, slot],
            d, mine,
        )

    def atom_copy(d, slot):
        return send(
            atom_send.at[d], atom_recv.at[slot], atom_ss.at[d], atom_rs.at[slot], d, mine
        )

    def up_copy(g, slot):
        return send(up_h.at[0], up_all.at[slot], up_ss.at[g], up_rs.at[slot], me, g)

    def low_copy(g, slot):
        return send(low_all.at[mine], low_all.at[slot], low_ss.at[g], low_rs.at[slot], me, g)

    def pair_copy(h, g, slot):
        return send(
            paired.at[h, g], pair_recv.at[h, slot], pair_ss.at[h, g], pair_rs.at[h, slot], me, g
        )

    parts = part_owner.shape[1]
    owner = part_owner[...]
    owner_col, rank_row, rank_col = ranks(owner)
    match = lines((n * seat, parts), 0) == owner * seat + rank_row
    goal = jnp.sum(
        jnp.where(match, part_target[...] + 1, 0), axis=1, keepdims=True
    )
    spread_goal = jnp.broadcast_to(goal - 1, (n * seat, 128))
    meta[:, 0:seat, :] = spread_goal.reshape(n, seat, 128)
    match = lines((parts, n * seat), 1) == owner_col * seat + rank_col
    items_v[...] = jnp.sum(
        jnp.where(match, lines((parts, n * seat), 0), 0), axis=0, keepdims=True
    )
    item_copy = pltpu.make_async_copy(items_v, items, item_sem.at[0])
    item_copy.start()

    slots = slot_owner.shape[1]
    owner = slot_owner[...]
    owner_col, rank_row, rank_col = ranks(owner)
    match = lines((n * acap, slots), 0) == owner * acap + rank_row
    held = jnp.sum(
        jnp.where(match, lines((n * acap, slots), 1) + 1, 0), axis=1, keepdims=True
    )
    pick[...] = (held - 1 == edge_slot[...]).astype(f32).astype(bf16)
    wanted = jnp.where(
        lines((n, slots), 0) == owner, slot_atom[...].astype(f32) + 1.0, 0.0
    ).astype(bf16)
    first_lane = me * acap
    lanes = (lines((slots, n * acap), 1) == rank_col + first_lane).astype(f32).astype(bf16)
    atom_meta = dot(wanted, lanes).astype(jnp.int32)
    for r in range(chunks):
        meta[:, seat + r, :] = atom_meta[:, r * 128 : (r + 1) * 128]

    loads[0].wait()
    loads[1].wait()
    projected = silu(dot(feats[...], pre[...])).astype(bf16)
    loads[2].wait()
    down_twice = jnp.concatenate([down[...], down[...]], axis=0)
    lowered = silu(
        lax.dot_general(
            projected, down_twice, (((1,), (1,)), ((), ())), preferred_element_type=f32
        )
    ).reshape(nb, 2, half, width)
    lane = lax.broadcasted_iota(jnp.int32, (nb, half, width), 2)
    low_all[mine] = jnp.where(lane < width // 2, lowered[:, 0], lowered[:, 1]).astype(bf16)

    pl.semaphore_wait(barrier, n - 1 + groups - 1)
    others = [lax.rem(mine + k, groups) for k in range(1, groups)]
    for g in others:
        low_copy(g, mine).start()

    def start_meta(k, carry):
        meta_copy(lax.rem(me + k, n), me).start()
        return carry

    lax.fori_loop(1, n, start_meta, 0)
    for g in others:
        up_copy(g, mine).start()
    meta_recv[me] = meta[me]

    def spread(g):
        lane = lax.broadcasted_iota(jnp.int32, (half, width), 1)
        left = lane < width // 2
        for i in range(nb):
            packed = low_all[g, i].astype(f32)
            turned = pltpu.roll(packed, width // 2, 1)
            at = g * nb + i
            diag[at, 0:half] = jnp.where(left, packed, 0.0).astype(bf16)
            diag[at, half : 2 * half] = jnp.where(left, turned, 0.0).astype(bf16)
            diag[at, 2 * half : 3 * half] = jnp.where(left, 0.0, turned).astype(bf16)
            diag[at, 3 * half :] = jnp.where(left, 0.0, packed).astype(bf16)

    spread(mine)
    loads[3].wait()
    for g in others:
        low_copy(g, g).wait_recv()
        spread(g)

    for p in range(parts):
        tile = angle[p, 0]
        wide = jnp.concatenate([tile[:half], tile[half:]], axis=1)
        prod[p] = dot(wide, diag[part_source[p]]).astype(bf16)
    item_copy.wait()

    pieces = part_send.shape[0]
    piece = half // pieces

    def fill(h, d, ref, slot):
        for s in range(cap):
            ref[h, slot, s] = prod[jnp.clip(items[0, d * seat + s], 0, prod.shape[0] - 1), h * piece : (h + 1) * piece]

    def start_part(h, k):
        d = lax.rem(me + k, n)
        fill(h, d, part_send, d)
        part_copy(h, d, me).start()

    for h in range(pieces):

        def start_two(i, carry):
            start_part(h, n // 2 + i)
            start_part(h, n // 2 - i)
            return carry

        start_part(h, n // 2)
        lax.fori_loop(1, n // 2, start_two, 0)
    for h in range(pieces):
        fill(h, me, part_recv, me)

    loads[4].wait()
    for g in others:
        up_copy(g, g).wait_recv()
    blank = jnp.zeros(up_all.shape[1:], bf16)
    above = jnp.concatenate([x for g in range(groups) for x in (up_all[g], blank)], axis=0)
    below = jnp.concatenate([x for g in range(groups) for x in (blank, up_all[g])], axis=0)
    for load in loads[5:]:
        load.wait()

    acc[...] = jnp.zeros_like(acc)

    def add(h, src):
        targets = [meta_recv[src, s : s + 1, :] for s in range(cap)]
        arrived = [part_recv[h, src, s].astype(f32) for s in range(cap)]
        for j in range(groups * nb):
            total = acc[h, j]
            for t, a in zip(targets, arrived):
                total = total + jnp.where(jnp.broadcast_to(t == j, a.shape), a, 0.0)
            acc[h, j] = total

    depth = above.shape[1]
    for h in range(pieces):
        add(h, me)

        def take(i, carry):
            src = lax.rem(me + i, n)
            if h == 0:
                meta_copy(src, src).wait_recv()
            part_copy(h, src, src).wait_recv()
            add(h, src)
            return carry

        lax.fori_loop(1, n, take, 0)
        for g in range(groups):
            paired[h, g] = acc[h, g * nb : (g + 1) * nb].reshape(nb * piece, width).astype(bf16)
        for g in others:
            pair_copy(h, g, mine).start()
        pair_recv[h, mine] = paired[h, mine]
        for g in others:
            pair_copy(h, g, g).wait_recv()

        columns = jnp.concatenate([pair_recv[h, g] for g in range(groups)], axis=1)
        upper = dot(columns, above).reshape(nb, 1, piece, depth)
        lower = dot(columns, below).reshape(nb, 1, piece, depth)
        triplet = jnp.concatenate([upper, lower], axis=1).reshape(2 * nb * piece, depth)
        starts = [q * half + h * piece for q in range(2 * nb)]
        own = jnp.concatenate([feats[at : at + piece] for at in starts], axis=0)
        joined = (own.astype(f32) + triplet).astype(bf16)
        inner = silu(dot(joined, first[...])).astype(bf16)
        deep = silu(dot(inner, second[...]))
        update = ((joined.astype(f32) + deep) * half_root).astype(bf16)
        for q, at in enumerate(starts):
            edge_out[at : at + piece] = update[q * piece : (q + 1) * piece]

    atom_send[...] = dot(pick[...], edge_out[...]).astype(bf16).reshape(atom_send.shape)

    def start_atom(i, carry):
        for k in (n // 2 + i, n // 2 - i):
            atom_copy(lax.rem(me + k, n), me).start()
        return carry

    atom_copy(lax.rem(me + n // 2, n), me).start()
    lax.fori_loop(1, n // 2, start_atom, 0)
    atom_recv[me] = atom_send[me]

    named = jnp.sum(meta_recv[...], axis=0)[seat:]
    atoms = afeats.shape[0]
    ids = lax.broadcasted_iota(jnp.int32, (atoms, 128), 0) + 1
    chosen = jnp.concatenate(
        [(ids == named[r : r + 1]).astype(f32).astype(bf16) for r in range(chunks)], axis=1
    )
    def take_atom(i, carry):
        src = lax.rem(me + i, n)
        atom_copy(src, src).wait_recv()
        return carry

    lax.fori_loop(1, n, take_atom, 0)
    gathered = dot(chosen, atom_recv[...].reshape(n * acap, atom_recv.shape[2])).astype(bf16)
    hidden = silu(dot(gathered, afirst[...])).astype(bf16)
    atom_out[...] = (afeats[...].astype(f32) + dot(hidden, asecond[...])).astype(bf16)

    def finish(k, carry):
        d = lax.rem(me + k, n)
        meta_copy(d, me).wait_send()
        for h in range(pieces):
            part_copy(h, d, me).wait_send()
        atom_copy(d, me).wait_send()
        return carry

    lax.fori_loop(1, n, finish, 0)
    for g in others:
        low_copy(g, mine).wait_send()
        up_copy(g, mine).wait_send()
        for h in range(pieces):
            pair_copy(h, g, mine).wait_send()


def body(
    edge_feats, pre_weight, down_weight, angle_tiles, part_source, part_owner, part_target,
    up_weight, res_first, res_second, edge_slot, slot_owner, slot_atom, atom_feats,
    atom_first, atom_second,
):
    n, groups = lax.axis_size("graph"), lax.axis_size("basis")
    parts, _, block, _ = angle_tiles.shape
    narrow = down_weight.shape[1]
    rows, wide = edge_feats.shape
    nb = rows // block
    slot_count = slot_owner.shape[1]
    cap = max(2, 2 * parts // n)
    acap = -(-max(2, 2 * slot_count // n) // 16) * 16

    seat = -(-cap // 8) * 8
    chunks = n * acap // 128
    meta_rows = seat + -(-chunks // 8) * 8
    pieces = 2

    half, pair_width = block // 2, 2 * narrow
    dma = pltpu.SemaphoreType.DMA
    vmem = pl.BlockSpec(memory_space=pltpu.VMEM)
    hbm = pl.BlockSpec(memory_space=pl.ANY)
    scratch = [
        pltpu.VMEM(edge_feats.shape, bf16),
        pltpu.VMEM(pre_weight.shape, bf16),
        pltpu.VMEM(down_weight.shape[::-1], bf16),
        pltpu.VMEM(angle_tiles.shape, bf16),
        pltpu.VMEM((groups,) + up_weight.shape[1:], bf16),
        pltpu.VMEM(res_first.shape, bf16),
        pltpu.VMEM(res_second.shape, bf16),
        pltpu.VMEM(atom_feats.shape, bf16),
        pltpu.VMEM(atom_first.shape, bf16),
        pltpu.VMEM(atom_second.shape, bf16),
        pltpu.VMEM((groups, nb, half, pair_width), bf16),
        pltpu.VMEM((groups * nb, 2 * block, pair_width), bf16),
        pltpu.VMEM((parts, half, pair_width), bf16),
        pltpu.VMEM((pieces, n, cap, half // pieces, pair_width), bf16),
        pltpu.VMEM((pieces, n, cap, half // pieces, pair_width), bf16),
        pltpu.VMEM((n, meta_rows, 128), jnp.int32),
        pltpu.VMEM((n, meta_rows, 128), jnp.int32),
        pltpu.VMEM((1, n * seat), jnp.int32),
        pltpu.SMEM((1, n * seat), jnp.int32),
        pltpu.VMEM((pieces, groups * nb, half // pieces, pair_width), f32),
        pltpu.VMEM((pieces, groups, nb * half // pieces, pair_width), bf16),
        pltpu.VMEM((pieces, groups, nb * half // pieces, pair_width), bf16),
        pltpu.VMEM((n * acap, rows), bf16),
        pltpu.VMEM((n, acap, wide), bf16),
        pltpu.VMEM((n, acap, wide), bf16),
        dma((10,)),
        dma((1,)),
    ]
    scratch += [dma((n,))] * 2 + [dma((pieces, n))] * 2 + [dma((n,))] * 2
    scratch += [dma((groups,))] * 4 + [dma((pieces, groups))] * 2
    return pl.pallas_call(
        functools.partial(kernel, n, groups, cap, acap, seat, chunks, nb, block),
        out_shape=(
            jax.ShapeDtypeStruct(edge_feats.shape, bf16),
            jax.ShapeDtypeStruct(atom_feats.shape, bf16),
        ),
        in_specs=[pl.BlockSpec(memory_space=pltpu.SMEM)] + [vmem] * 5 + [hbm] * 10,
        out_specs=(vmem, vmem),
        scratch_shapes=scratch,
        compiler_params=pltpu.CompilerParams(
            collective_id=0, has_side_effects=True, vmem_limit_bytes=62 * 2**20
        ),
    )(
        part_source, part_owner.reshape(1, parts), part_target.reshape(1, parts),
        slot_owner.reshape(1, slot_count), slot_atom, edge_slot,
        edge_feats, pre_weight, down_weight.T,
        angle_tiles, up_weight, res_first, res_second, atom_feats, atom_first, atom_second,
    )


def solution(mesh):
    rows = P(("graph", "basis"), None)
    in_specs = (
        rows,
        P(),
        P(),
        P("graph", "basis", None, None),
        P("graph"),
        P("graph", None),
        P("graph"),
        P("basis", None, None),
        P(),
        P(),
        rows,
        P(("graph", "basis"), None, None),
        rows,
        rows,
        P(),
        P(),
    )
    return jax.shard_map(
        body, mesh=mesh, in_specs=in_specs, out_specs=(rows, rows), check_vma=False
    )
```

time: 58.5 us -> 46.7 us (0.80)
  local copies, waits for them, and re-layouts: 9.41 us -> 2.49 us
  other arithmetic: 5.6 us -> 0 us
  Pallas kernels: 42.2 us -> 43.4 us
    unnamed x23 -> x4, local copies, waits for them, and re-layouts: 8.66 us -> 2.49 us
    reduce_sum x4 -> x0, other arithmetic: 2.06 us -> none  [the longest x2 1.81 us: slot_table(): rank = jnp.sum(same.astype(jnp.int32), axis=1)]
    add x4 -> x0, other arithmetic: 2.05 us -> none  [the longest x1 0.73 us: slot_table(): picked = jnp.sum(jnp.where(match, values[None, :] + 1, 0), axis=1) - 1]
    pallas_call x1, Pallas kernels: 42.2 us -> 43.4 us  [body(): pl.pallas_call(functools.partial(kernel, n, groups, cap, acap, seat, chun...]
    concatenate x2 -> x0, other arithmetic: 0.81 us -> none  [the longest x1 0.73 us: body(): scal = jnp.concatenate([part_source, jnp.maximum(items, 0)])]
    broadcast_in_dim x1 -> x0, other arithmetic: 0.66 us -> none  [slot_table(): picked = jnp.sum(jnp.where(match, values[None, :] + 1, 0), axis=1) - 1]
where the time goes in v2:
time: 46.7 us; the launch traced here: 46.5 us
  Pallas kernels  43.4 us (93%)
  local copies, waits for them, and re-layouts  2.49 us (5%)
  between operations  0.65 us (1%)
    pallas_call x1, Pallas kernels, body(): pl.pallas_call(functools.partial(kernel, n, groups, cap, acap, seat, chun...  43.4 us
    unnamed x4, local copies, waits for them, and re-layouts  2.49 us

profile of v2, /device:TPU:0, one launch (start us, length us, event | category | flops | bytes accessed | tf_op | source)
XLA Modules:
  0.0 46.5 jit_solution(16831739531221114167)
XLA Ops:
  0.6 43.4 %shard_map.167 = (bf16[512,512]{1,0:T(8,128)(2,1)}, bf16[32,512]{1,0:T(8,128)(2,1)}) custom-call(s32[24]{0:T(128)} %part_source.1, s32[1,24]{1,0:T(1,128)} %bitcast.5, s32[1,24]{1,0:T(1,128)} %bitcast.6, s32[1,128]{1,0:T(1,128)} %bitcast.7, s32[1,128]{1,0:T(1,128)} %slot_atom.1, s32[1,512]{1,0:T(1,128)} %edge_slot.1, bf16[512,512]{1,0:T(8,128)(2,1)} %feats_h.1, ...), custom_call_target="tpu_custom_call" | custom-call | tf_op jit(solution)/shard_map/pallas_call | solution.py:371
  44.0 0.0 copy-start
  44.0 1.9 %copy.20 = bf16[512,512]{1,0:T(8,128)(2,1)} copy(bf16[512,512]{1,0:T(8,128)(2,1)} %get-tuple-element.4) | data formatting | bytes 1048576
  45.9 0.0 copy-done
  45.9 0.6 %copy.21 = bf16[32,512]{1,0:T(8,128)(2,1)} copy(bf16[32,512]{1,0:T(8,128)(2,1)S(1)} %copy-done) | data formatting | bytes 65536
Async XLA Ops:
  44.0 1.9 %copy-start = (bf16[32,512]{1,0:T(8,128)(2,1)S(1)}, bf16[32,512]{1,0:T(8,128)(2,1)}, u32[]{:S(2)}) copy-start(bf16[32,512]{1,0:T(8,128)(2,1)} %get-tuple-element.5) | copy-start | bytes 98308
